TPU v7x, 32 devices: a whole 2x2x4 slice. The times are simulated.
32 devices in a mesh: seq: 4 (over y, x), head: 8 (over z, core).
Axes of the slice: x: 2, y: 2, z: 4, core: 2. Of those that a mesh axis runs over, the one named last changes fastest.
Arguments:
- grad_out: float32 [4096, 1024], P(('seq', 'head')), may hold values from -0.03125 to 0.03125
- features: float32 [4096, 1024], P(('seq', 'head')), may hold values from -6 to 6
- step_size: float32 [4096, 16], P(('seq', 'head')), may hold values from 0.3 to 3
- log_decay: float32 [4096, 16], P(('seq', 'head')), may hold values from -0.85 to 0
- write_proj: float32 [4096, 8, 128], P(('seq', 'head')), may hold values from -6 to 6
- read_proj: float32 [4096, 8, 128], P(('seq', 'head')), may hold values from -6 to 6
Outputs:
- grad_features: float32 [4096, 1024], P(('seq', 'head'))
- grad_write: float32 [4096, 8, 128], P(('seq', 'head'))
- read_gradient: float32 [4096, 8, 128], P(('seq', 'head'))
All inputs are finite; a program needn't handle non-finite values.
Results may differ from a plain program's by a relative error of at most 0.00015.
Values sent between devices are 32-bit elements; how exact they have to be, the bound alone decides.
A program may use at most 64 MiB of HBM per device.

v0:
```python
import jax
import jax.numpy as jnp
from jax import lax
from jax.sharding import PartitionSpec as P

SPAN = 256


PRECISE = lax.Precision.HIGHEST


def shifted(block, axis, distance):
    devices = range(lax.axis_size(axis))
    route = [(i - distance, i) for i in devices if i - distance in devices]
    return lax.ppermute(block, axis, route)


def span_summary(feat_here, step_here, decay_here, write_here):
    cum_log = jnp.cumsum(decay_here, axis=1)
    end_log = cum_log[:, -1]
    weight_in = step_here * jnp.exp(end_log[:, None, :] - cum_log)
    fwd_state = jnp.einsum(
        "cqn,cqhp->chnp", write_here, feat_here * weight_in[..., None], precision=PRECISE
    )
    return (cum_log, end_log, fwd_state)


def adjoint_summary(grad_here, read_here, cum_log):
    return jnp.einsum(
        "cqn,cqhp->chnp", read_here, grad_here * jnp.exp(cum_log)[..., None], precision=PRECISE
    )


def advance(running, element):
    decay_now, local_now = element
    return (decay_now[:, None, None] * running + local_now, running)


def span_grads(
    feat_here, grad_here, step_here, cum_log, end_log, write_here, read_here, enters, leaves
):
    length = feat_here.shape[1]
    cum_turned = jnp.swapaxes(cum_log, 1, 2)
    step_turned = jnp.swapaxes(step_here, 1, 2)
    element_offset_along = jnp.arange(length)
    causal = element_offset_along[:, None] >= element_offset_along[None, :]
    decay_mat = jnp.exp(
        jnp.where(causal, cum_turned[:, :, :, None] - cum_turned[:, :, None, :], -jnp.inf)
    )
    products = jnp.einsum("cthp,cshp->chts", grad_here, feat_here, precision=PRECISE) * decay_mat
    matches = (
        jnp.einsum("ctn,csn->cts", read_here, write_here, precision=PRECISE)[:, None] * decay_mat
    )
    weighted = products * step_turned[:, :, None, :]
    to_end = jnp.exp(end_log[:, None, :] - cum_log)
    read_grad = jnp.einsum("chts,csn->ctn", weighted, write_here, precision=PRECISE)
    read_grad = read_grad + jnp.einsum(
        "cthp,chnp->ctn", grad_here * jnp.exp(cum_log)[..., None], enters, precision=PRECISE
    )
    write_grad = jnp.einsum("chts,ctn->csn", weighted, read_here, precision=PRECISE)
    write_grad = write_grad + jnp.einsum(
        "cshp,chnp->csn", feat_here * (to_end * step_here)[..., None], leaves, precision=PRECISE
    )
    feat_grad = jnp.einsum("chts,cthp->cshp", matches, grad_here, precision=PRECISE)
    feat_grad = feat_grad + to_end[..., None] * jnp.einsum(
        "csn,chnp->cshp", write_here, leaves, precision=PRECISE
    )
    feat_grad = feat_grad * step_here[..., None]
    return (feat_grad, write_grad, read_grad)


def shards(grad_out, features, step_size, log_decay, write_proj, read_proj):
    owners = lax.axis_size("head")
    rows_in = grad_out.shape[0]
    my_heads = step_size.shape[1] // owners
    head_cols = grad_out.shape[1] // owners
    head_size = head_cols // my_heads
    groups = write_proj.shape[1]
    state_dim = write_proj.shape[2]
    repeats = owners // groups
    seg_rows = rows_in * owners
    span_len = min(SPAN, seg_rows)
    num_spans = seg_rows // span_len
    outbound_gradient = grad_out.reshape(rows_in, owners, head_cols)
    feat_send = features.reshape(rows_in, owners, head_cols)
    step_send = step_size.reshape(rows_in, owners, my_heads)
    decay_send = log_decay.reshape(rows_in, owners, my_heads)
    outbound_write = jnp.repeat(write_proj, repeats, axis=1)
    read_send = jnp.repeat(read_proj, repeats, axis=1)
    head_shape = (num_spans, span_len, my_heads, head_size)
    incoming_slope_share, feat_recv, step_recv, decay_recv, write_recv, read_recv = (
        lax.all_to_all(outbound_gradient, "head", split_axis=1, concat_axis=0, tiled=True),
        lax.all_to_all(feat_send, "head", split_axis=1, concat_axis=0, tiled=True),
        lax.all_to_all(step_send, "head", split_axis=1, concat_axis=0, tiled=True),
        lax.all_to_all(decay_send, "head", split_axis=1, concat_axis=0, tiled=True),
        lax.all_to_all(outbound_write, "head", split_axis=1, concat_axis=0, tiled=True),
        lax.all_to_all(read_send, "head", split_axis=1, concat_axis=0, tiled=True),
    )
    feat_here = feat_recv.reshape(head_shape)
    step_here = step_recv.reshape(num_spans, span_len, my_heads)
    write_here = write_recv.reshape(num_spans, span_len, state_dim)
    cum_log, end_log, fwd_state = span_summary(
        feat_here, step_here, decay_recv.reshape(num_spans, span_len, my_heads), write_here
    )
    grad_here = incoming_slope_share.reshape(head_shape)
    read_here = read_recv.reshape(num_spans, span_len, state_dim)
    adj_state = adjoint_summary(grad_here, read_here, cum_log)
    decay_ratio = jnp.exp(end_log)
    zero_state = jnp.zeros((my_heads, state_dim, head_size), jnp.float32)
    dev_fwd, local_enters = lax.scan(advance, zero_state, (decay_ratio, fwd_state))
    dev_adj, local_leaves = lax.scan(advance, zero_state, (decay_ratio, adj_state), reverse=True)
    log_upto = jnp.cumsum(end_log, axis=0)
    dev_log = log_upto[-1]
    dev_decay = jnp.exp(dev_log)
    segment_owner_count = lax.axis_size("seq")

    def relay_turn(turn_idx, pair):
        from_low, from_high = pair
        from_low = shifted(dev_decay[:, None, None] * from_low + dev_fwd, "seq", 1)
        from_high = shifted(dev_decay[:, None, None] * from_high + dev_adj, "seq", -1)
        return (from_low, from_high)

    incoming, outgoing = lax.fori_loop(
        0, segment_owner_count - 1, relay_turn, (zero_state, zero_state)
    )
    enters = local_enters + jnp.exp(log_upto - end_log)[:, :, None, None] * incoming[None]
    leaves = local_leaves + jnp.exp(dev_log[None, :] - log_upto)[:, :, None, None] * outgoing[None]
    feat_grad, write_grad, read_grad = span_grads(
        feat_here, grad_here, step_here, cum_log, end_log, write_here, read_here, enters, leaves
    )
    feat_back, write_back, read_back = (
        lax.all_to_all(
            feat_grad.reshape(seg_rows, 1, head_cols),
            "head",
            split_axis=0,
            concat_axis=1,
            tiled=True,
        ),
        lax.all_to_all(
            write_grad.reshape(seg_rows, 1, state_dim),
            "head",
            split_axis=0,
            concat_axis=1,
            tiled=True,
        ),
        lax.all_to_all(
            read_grad.reshape(seg_rows, 1, state_dim),
            "head",
            split_axis=0,
            concat_axis=1,
            tiled=True,
        ),
    )
    grad_features = feat_back.reshape(rows_in, owners * head_cols)
    grad_write = write_back.reshape(rows_in, groups, repeats, state_dim).sum(axis=2)
    read_gradient = read_back.reshape(rows_in, groups, repeats, state_dim).sum(axis=2)
    return (grad_features, grad_write, read_gradient)


def solution(mesh):
    placed = (
        P(("seq", "head"), None),
        P(("seq", "head"), None),
        P(("seq", "head"), None),
        P(("seq", "head"), None),
        P(("seq", "head"), None, None),
        P(("seq", "head"), None, None),
    )
    return jax.shard_map(
        shards,
        mesh=mesh,
        in_specs=placed,
        out_specs=(
            P(("seq", "head"), None),
            P(("seq", "head"), None, None),
            P(("seq", "head"), None, None),
        ),
        check_vma=False,
    )
```

profile of v0, /device:TPU:0, one launch (start us, length us, event | category | flops | bytes accessed | tf_op | source)
XLA Modules:
  0.0 198.1 jit_solution(4487265107094055519)
XLA Ops:
  0.6 11.9 %all_to_all.135 = f32[128,8,2]{0,2,1:T(2,128)S(1)} all-to-all(f32[128,8,2]{0,2,1:T(2,128)} %bitcast.154), channel_id=1, replica_groups=mesh['seq'=4,'head'=8] {'head'}, dimensions={1} | all-to-all | bytes 16384 | tf_op jit(solution)/shard_map/all_to_all | solution.py:95
  18.0 3.4 %all-to-all-done.5 = f32[128,8,2]{0,2,1:T(2,128)S(1)} async-done(((f32[128,8,2]{0,2,1:T(2,128)}), f32[128,8,2]{0,2,1:T(2,128)S(1)}, u32[]{:S(2)}, u32[]{:S(2)}) %all-to-all-start.5) | async-done | bytes 8224 | tf_op jit(solution)/shard_map/all_to_all | solution.py:94
  21.4 3.5 %all-to-all-start.3 = ((f32[128,8,128]{0,2,1:T(8,128)}), f32[128,8,128]{0,2,1:T(8,128)S(1)}, u32[]{:S(2)}, u32[]{:S(2)}) async-start(f32[128,8,128]{0,2,1:T(8,128)} %bitcast.12), calls=%async_computation.3 | async-start | bytes 1048576 | tf_op jit(solution)/shard_map/all_to_all | solution.py:92
  26.0 14.3 %all-to-all-done.3 = f32[128,8,128]{0,2,1:T(8,128)S(1)} async-done(((f32[128,8,128]{0,2,1:T(8,128)}), f32[128,8,128]{0,2,1:T(8,128)S(1)}, u32[]{:S(2)}, u32[]{:S(2)}) %all-to-all-start.3) | async-done | bytes 524320 | tf_op jit(solution)/shard_map/all_to_all | solution.py:92
  40.2 3.6 %all-to-all-start.4 = ((f32[128,8,128]{0,2,1:T(8,128)}), f32[128,8,128]{0,2,1:T(8,128)S(1)}, u32[]{:S(2)}, u32[]{:S(2)}) async-start(f32[128,8,128]{0,2,1:T(8,128)} %bitcast.22), calls=%async_computation.4 | async-start | bytes 1048576 | tf_op jit(solution)/shard_map/all_to_all | solution.py:93
  48.6 10.5 %all-to-all-done.4 = f32[128,8,128]{0,2,1:T(8,128)S(1)} async-done(((f32[128,8,128]{0,2,1:T(8,128)}), f32[128,8,128]{0,2,1:T(8,128)S(1)}, u32[]{:S(2)}, u32[]{:S(2)}) %all-to-all-start.4) | async-done | bytes 524320 | tf_op jit(solution)/shard_map/all_to_all | solution.py:93
  59.1 3.5 %all-to-all-start.1 = ((f32[128,8,128]{2,0,1:T(8,128)}), f32[128,8,128]{2,0,1:T(8,128)S(1)}, u32[]{:S(2)}, u32[]{:S(2)}) async-start(f32[128,8,128]{2,0,1:T(8,128)} %copy.96), calls=%async_computation.1 | async-start | bytes 1048576 | tf_op jit(solution)/shard_map/all_to_all | solution.py:96
  65.5 12.4 %all-to-all-done.1 = f32[128,8,128]{2,0,1:T(8,128)S(1)} async-done(((f32[128,8,128]{2,0,1:T(8,128)}), f32[128,8,128]{2,0,1:T(8,128)S(1)}, u32[]{:S(2)}, u32[]{:S(2)}) %all-to-all-start.1) | async-done | bytes 524320 | tf_op jit(solution)/shard_map/all_to_all | solution.py:96
  77.9 3.5 %all-to-all-start = ((f32[128,8,128]{2,0,1:T(8,128)}), f32[128,8,128]{2,0,1:T(8,128)S(1)}, u32[]{:S(2)}, u32[]{:S(2)}) async-start(f32[128,8,128]{2,0,1:T(8,128)} %copy.95), calls=%async_computation | async-start | bytes 1048576 | tf_op jit(solution)/shard_map/all_to_all | solution.py:97
  83.2 13.5 %all-to-all-done = f32[128,8,128]{2,0,1:T(8,128)S(1)} async-done(((f32[128,8,128]{2,0,1:T(8,128)}), f32[128,8,128]{2,0,1:T(8,128)S(1)}, u32[]{:S(2)}, u32[]{:S(2)}) %all-to-all-start) | async-done | bytes 524320 | tf_op jit(solution)/shard_map/all_to_all | solution.py:97
  98.5 4.6 %multiply_reduce_fusion = f32[4,256,256]{2,1,0:T(8,128)} fusion(f32[4,2,256]{2,1,0:T(2,128)S(1)} %copy.121, f32[4,2,256]{2,1,0:T(2,128)S(1)} %reduce_window_sum.35, pred[256,256]{1,0:T(8,128)(4,1)S(1)} %iota_compare_fusion, f32[4,256,2,64]{1,0,3,2:T(4,128)} %copy-done.3, f32[4,256,2,64]{1,0,3,2:T(4,128)} %copy-done.1), kind=kOutput, calls=%fused_computation.12 | convolution fusion | flops 405012480 | bytes 2179072 | tf_op jit(solution)/shard_map/cthp,cshp->chts/dot_general | solution.py:50
  103.2 32.4 %while.42 = (s32[]{:T(128)}, f32[2,128,64]{2,1,0:T(8,128)S(1)}, f32[2,128,64]{2,1,0:T(8,128)S(1)}, f32[2]{0:T(128)S(1)}, f32[2,128,64]{2,1,0:T(8,128)S(1)}, /*index=5*/f32[2,128,64]{2,1,0:T(8,128)S(1)}, s32[]{:T(128)}) while((s32[]{:T(128)}, f32[2,128,64]{2,1,0:T(8,128)S(1)}, f32[2,128,64]{2,1,0:T(8,128)S(1)}, f32[2]{0:T(128)S(1)}, ...), condition=%wide.region_8.9_spmd, body=%wide.region_7.8_spmd.sunk | while | flops 65538 | bytes 917669 | solution.py:123
  109.2 4.8 %collective-permute-done.1 = f32[2,128,64]{2,1,0:T(8,128)S(1)} collective-permute-done((f32[2,128,64]{2,1,0:T(8,128)S(1)}, f32[2,128,64]{2,1,0:T(8,128)S(1)}, u32[]{:S(2)}, u32[]{:S(2)}) %collective-permute-start.1) | collective-permute-done | bytes 65568 | tf_op jit(solution)/shard_map/while/body/eval_jaxpr/ppermute | solution.py:15
  114.1 3.9 %collective-permute-start = (f32[2,128,64]{2,1,0:T(8,128)S(1)}, f32[2,128,64]{2,1,0:T(8,128)S(1)}, u32[]{:S(2)}, u32[]{:S(2)}) collective-permute-start(f32[2,128,64]{2,1,0:T(8,128)S(1)} %get-tuple-element.392), channel_id=1, source_target_pairs={{0,8},{8,16},{16,24},{1,9},{9,17},{17,25},{2,10},{10,18},{18,26},{... | collective-permute-start | bytes 196616 | tf_op jit(solution)/shard_map/while/body/eval_jaxpr/ppermute | solution.py:15
  120.5 4.4 %collective-permute-done.1 = f32[2,128,64]{2,1,0:T(8,128)S(1)} collective-permute-done((f32[2,128,64]{2,1,0:T(8,128)S(1)}, f32[2,128,64]{2,1,0:T(8,128)S(1)}, u32[]{:S(2)}, u32[]{:S(2)}) %collective-permute-start.1) | collective-permute-done | bytes 65568 | tf_op jit(solution)/shard_map/while/body/eval_jaxpr/ppermute | solution.py:15
  124.9 3.8 %collective-permute-start = (f32[2,128,64]{2,1,0:T(8,128)S(1)}, f32[2,128,64]{2,1,0:T(8,128)S(1)}, u32[]{:S(2)}, u32[]{:S(2)}) collective-permute-start(f32[2,128,64]{2,1,0:T(8,128)S(1)} %get-tuple-element.392), channel_id=1, source_target_pairs={{0,8},{8,16},{16,24},{1,9},{9,17},{17,25},{2,10},{10,18},{18,26},{... | collective-permute-start | bytes 196616 | tf_op jit(solution)/shard_map/while/body/eval_jaxpr/ppermute | solution.py:15
  131.2 4.4 %collective-permute-done.1 = f32[2,128,64]{2,1,0:T(8,128)S(1)} collective-permute-done((f32[2,128,64]{2,1,0:T(8,128)S(1)}, f32[2,128,64]{2,1,0:T(8,128)S(1)}, u32[]{:S(2)}, u32[]{:S(2)}) %collective-permute-start.1) | collective-permute-done | bytes 65568 | tf_op jit(solution)/shard_map/while/body/eval_jaxpr/ppermute | solution.py:15
  140.5 3.7 %all-to-all-start.8 = ((f32[1024,1,128]{2,1,0:T(1,128)}), f32[1024,1,128]{2,1,0:T(1,128)S(1)}, u32[]{:S(2)}, u32[]{:S(2)}) async-start(f32[1024,1,128]{2,1,0:T(1,128)} %bitcast.49), calls=%async_computation.8 | async-start | bytes 1048576 | tf_op jit(solution)/shard_map/all_to_all | solution.py:146
  146.2 3.9 %convolution_add_fusion.1 = f32[4,256,128]{2,1,0:T(8,128)} fusion(f32[4,256,128]{2,1,0:T(8,128)S(1)} %convolution_bitcast_fusion.1, f32[4,256,256]{2,1,0:T(8,128)} %multiply_reduce_fusion, f32[4,256,128]{2,1,0:T(8,128)S(1)} %bitcast.140), kind=kOutput, calls=%fused_computation.17 | convolution fusion | flops 402784256 | bytes 2621440 | tf_op jit(solution)/shard_map/chts,ctn->csn/dot_general | solution.py:60
  150.1 9.2 %all-to-all-done.8 = f32[1024,1,128]{2,1,0:T(1,128)S(1)} async-done(((f32[1024,1,128]{2,1,0:T(1,128)}), f32[1024,1,128]{2,1,0:T(1,128)S(1)}, u32[]{:S(2)}, u32[]{:S(2)}) %all-to-all-start.8) | async-done | bytes 524320 | tf_op jit(solution)/shard_map/all_to_all | solution.py:146
  159.3 3.5 %all-to-all-start.7 = ((f32[1024,1,128]{2,1,0:T(1,128)}), f32[1024,1,128]{2,1,0:T(1,128)S(1)}, u32[]{:S(2)}, u32[]{:S(2)}) async-start(f32[1024,1,128]{2,1,0:T(1,128)} %bitcast.42), calls=%async_computation.7 | async-start | bytes 1048576 | tf_op jit(solution)/shard_map/all_to_all | solution.py:139
  169.4 8.7 %all-to-all-done.7 = f32[1024,1,128]{2,1,0:T(1,128)S(1)} async-done(((f32[1024,1,128]{2,1,0:T(1,128)}), f32[1024,1,128]{2,1,0:T(1,128)S(1)}, u32[]{:S(2)}, u32[]{:S(2)}) %all-to-all-start.7) | async-done | bytes 524320 | tf_op jit(solution)/shard_map/all_to_all | solution.py:139
  178.1 3.5 %all-to-all-start.6 = ((f32[1024,1,128]{2,1,0:T(1,128)}), f32[1024,1,128]{2,1,0:T(1,128)S(1)}, u32[]{:S(2)}, u32[]{:S(2)}) async-start(f32[1024,1,128]{2,1,0:T(1,128)} %reshape.151), calls=%async_computation.6 | async-start | bytes 1048576 | tf_op jit(solution)/shard_map/all_to_all | solution.py:132
  183.8 13.1 %all-to-all-done.6 = f32[1024,1,128]{2,1,0:T(1,128)S(1)} async-done(((f32[1024,1,128]{2,1,0:T(1,128)}), f32[1024,1,128]{2,1,0:T(1,128)S(1)}, u32[]{:S(2)}, u32[]{:S(2)}) %all-to-all-start.6) | async-done | bytes 524320 | tf_op jit(solution)/shard_map/all_to_all | solution.py:132
  (122 shorter events, 47.4 us)
Async XLA Ops:
  12.6 8.9 %all-to-all-start.5 = ((f32[128,8,2]{0,2,1:T(2,128)}), f32[128,8,2]{0,2,1:T(2,128)S(1)}, u32[]{:S(2)}, u32[]{:S(2)}) async-start(f32[128,8,2]{0,2,1:T(2,128)} %bitcast.155), calls=%async_computation.5 | async-start | bytes 16384 | tf_op jit(solution)/shard_map/all_to_all | solution.py:94
  15.9 9.0 %copy-start.5 = (f32[128,1024]{1,0:T(8,128)S(1)}, f32[128,1024]{1,0:T(8,128)}, u32[]{:S(2)}) copy-start(f32[128,1024]{1,0:T(8,128)} %param.13) | copy-start | bytes 1572868
  21.4 18.8 %all-to-all-start.3 = ((f32[128,8,128]{0,2,1:T(8,128)}), f32[128,8,128]{0,2,1:T(8,128)S(1)}, u32[]{:S(2)}, u32[]{:S(2)}) async-start(f32[128,8,128]{0,2,1:T(8,128)} %bitcast.12), calls=%async_computation.3 | async-start | bytes 1048576 | tf_op jit(solution)/shard_map/all_to_all | solution.py:92
  25.0 18.9 %copy-start.6 = (f32[128,8,128]{2,1,0:T(8,128)S(1)}, f32[128,8,128]{2,1,0:T(8,128)}, u32[]{:S(2)}) copy-start(f32[128,8,128]{2,1,0:T(8,128)} %param.16) | copy-start | bytes 1572868
  40.2 4.6 %copy-start.7 = (f32[128,8,128]{2,1,0:T(8,128)S(1)}, f32[128,8,128]{2,1,0:T(8,128)}, u32[]{:S(2)}) copy-start(f32[128,8,128]{2,1,0:T(8,128)} %param.17) | copy-start | bytes 1572868
  40.2 18.9 %all-to-all-start.4 = ((f32[128,8,128]{0,2,1:T(8,128)}), f32[128,8,128]{0,2,1:T(8,128)S(1)}, u32[]{:S(2)}, u32[]{:S(2)}) async-start(f32[128,8,128]{0,2,1:T(8,128)} %bitcast.22), calls=%async_computation.4 | async-start | bytes 1048576 | tf_op jit(solution)/shard_map/all_to_all | solution.py:93
  59.1 18.8 %all-to-all-start.1 = ((f32[128,8,128]{2,0,1:T(8,128)}), f32[128,8,128]{2,0,1:T(8,128)S(1)}, u32[]{:S(2)}, u32[]{:S(2)}) async-start(f32[128,8,128]{2,0,1:T(8,128)} %copy.96), calls=%async_computation.1 | async-start | bytes 1048576 | tf_op jit(solution)/shard_map/all_to_all | solution.py:96
  64.1 0.8 copy-start.1
  64.7 0.8 copy-start.3
  77.9 18.8 %all-to-all-start = ((f32[128,8,128]{2,0,1:T(8,128)}), f32[128,8,128]{2,0,1:T(8,128)S(1)}, u32[]{:S(2)}, u32[]{:S(2)}) async-start(f32[128,8,128]{2,0,1:T(8,128)} %copy.95), calls=%async_computation | async-start | bytes 1048576 | tf_op jit(solution)/shard_map/all_to_all | solution.py:97
  83.2 13.5 %copy-start.4 = (f32[4,2,128,64]{3,2,1,0:T(8,128)}, f32[4,2,128,64]{3,2,1,0:T(8,128)S(1)}, u32[]{:S(2)}) copy-start(f32[4,2,128,64]{3,2,1,0:T(8,128)S(1)} %get-tuple-element.172) | copy-start | bytes 786436
  103.3 5.9 %collective-permute-start = (f32[2,128,64]{2,1,0:T(8,128)S(1)}, f32[2,128,64]{2,1,0:T(8,128)S(1)}, u32[]{:S(2)}, u32[]{:S(2)}) collective-permute-start(f32[2,128,64]{2,1,0:T(8,128)S(1)} %get-tuple-element.392), channel_id=1, source_target_pairs={{0,8},{8,16},{16,24},{1,9},{9,17},{17,25},{2,10},{10,18},{18,26},{... | collective-permute-start | bytes 196616 | tf_op jit(solution)/shard_map/while/body/eval_jaxpr/ppermute | solution.py:15
  106.7 7.3 %collective-permute-start.1 = (f32[2,128,64]{2,1,0:T(8,128)S(1)}, f32[2,128,64]{2,1,0:T(8,128)S(1)}, u32[]{:S(2)}, u32[]{:S(2)}) collective-permute-start(f32[2,128,64]{2,1,0:T(8,128)S(1)} %get-tuple-element.393), channel_id=1, source_target_pairs={{8,0},{16,8},{24,16},{9,1},{17,9},{25,17},{10,2},{18,10},{26,18},{... | collective-permute-start | bytes 196616 | tf_op jit(solution)/shard_map/while/body/eval_jaxpr/ppermute | solution.py:15
  114.1 6.4 %collective-permute-start = (f32[2,128,64]{2,1,0:T(8,128)S(1)}, f32[2,128,64]{2,1,0:T(8,128)S(1)}, u32[]{:S(2)}, u32[]{:S(2)}) collective-permute-start(f32[2,128,64]{2,1,0:T(8,128)S(1)} %get-tuple-element.392), channel_id=1, source_target_pairs={{0,8},{8,16},{16,24},{1,9},{9,17},{17,25},{2,10},{10,18},{18,26},{... | collective-permute-start | bytes 196616 | tf_op jit(solution)/shard_map/while/body/eval_jaxpr/ppermute | solution.py:15
  118.0 6.9 %collective-permute-start.1 = (f32[2,128,64]{2,1,0:T(8,128)S(1)}, f32[2,128,64]{2,1,0:T(8,128)S(1)}, u32[]{:S(2)}, u32[]{:S(2)}) collective-permute-start(f32[2,128,64]{2,1,0:T(8,128)S(1)} %get-tuple-element.393), channel_id=1, source_target_pairs={{8,0},{16,8},{24,16},{9,1},{17,9},{25,17},{10,2},{18,10},{26,18},{... | collective-permute-start | bytes 196616 | tf_op jit(solution)/shard_map/while/body/eval_jaxpr/ppermute | solution.py:15
  124.9 6.3 %collective-permute-start = (f32[2,128,64]{2,1,0:T(8,128)S(1)}, f32[2,128,64]{2,1,0:T(8,128)S(1)}, u32[]{:S(2)}, u32[]{:S(2)}) collective-permute-start(f32[2,128,64]{2,1,0:T(8,128)S(1)} %get-tuple-element.392), channel_id=1, source_target_pairs={{0,8},{8,16},{16,24},{1,9},{9,17},{17,25},{2,10},{10,18},{18,26},{... | collective-permute-start | bytes 196616 | tf_op jit(solution)/shard_map/while/body/eval_jaxpr/ppermute | solution.py:15
  128.7 6.9 %collective-permute-start.1 = (f32[2,128,64]{2,1,0:T(8,128)S(1)}, f32[2,128,64]{2,1,0:T(8,128)S(1)}, u32[]{:S(2)}, u32[]{:S(2)}) collective-permute-start(f32[2,128,64]{2,1,0:T(8,128)S(1)} %get-tuple-element.393), channel_id=1, source_target_pairs={{8,0},{16,8},{24,16},{9,1},{17,9},{25,17},{10,2},{18,10},{26,18},{... | collective-permute-start | bytes 196616 | tf_op jit(solution)/shard_map/while/body/eval_jaxpr/ppermute | solution.py:15
  135.6 3.1 %copy-start = (f32[4,256,256]{2,1,0:T(8,128)S(1)}, f32[4,256,256]{2,1,0:T(8,128)}, u32[]{:S(2)}) copy-start(f32[4,256,256]{2,1,0:T(8,128)} %multiply_reduce_fusion) | copy-start | bytes 3145732
  140.5 18.8 %all-to-all-start.8 = ((f32[1024,1,128]{2,1,0:T(1,128)}), f32[1024,1,128]{2,1,0:T(1,128)S(1)}, u32[]{:S(2)}, u32[]{:S(2)}) async-start(f32[1024,1,128]{2,1,0:T(1,128)} %bitcast.49), calls=%async_computation.8 | async-start | bytes 1048576 | tf_op jit(solution)/shard_map/all_to_all | solution.py:146
  159.3 18.8 %all-to-all-start.7 = ((f32[1024,1,128]{2,1,0:T(1,128)}), f32[1024,1,128]{2,1,0:T(1,128)S(1)}, u32[]{:S(2)}, u32[]{:S(2)}) async-start(f32[1024,1,128]{2,1,0:T(1,128)} %bitcast.42), calls=%async_computation.7 | async-start | bytes 1048576 | tf_op jit(solution)/shard_map/all_to_all | solution.py:139
  162.8 1.0 copy-start.2
  178.1 18.8 %all-to-all-start.6 = ((f32[1024,1,128]{2,1,0:T(1,128)}), f32[1024,1,128]{2,1,0:T(1,128)S(1)}, u32[]{:S(2)}, u32[]{:S(2)}) async-start(f32[1024,1,128]{2,1,0:T(1,128)} %reshape.151), calls=%async_computation.6 | async-start | bytes 1048576 | tf_op jit(solution)/shard_map/all_to_all | solution.py:132
where the time goes:
time: 199 us; the launch traced here: 198 us
  waiting for transfers between devices  102 us (51%)
  starting transfers between devices  43 us (22%)
  matrix products  20.8 us (10%)
  local copies, waits for them, and re-layouts  14.6 us (7%)
  blocking collectives  11.9 us (6%)
  other arithmetic  4.14 us (2%)
    ppermute x6, waiting for transfers between devices, shifted(): return lax.ppermute(block, axis, route)  17.1 us
    ppermute x6, starting transfers between devices, shifted(): return lax.ppermute(block, axis, route)  14.9 us
    all_to_all x1, waiting for transfers between devices, shards(): lax.all_to_all(outbound_gradient, 'head', split_axis=1, concat_axis=0, ti...  14.3 us
    all_to_all x1, waiting for transfers between devices, shards(): lax.all_to_all(read_send, 'head', split_axis=1, concat_axis=0, tiled=True)  13.5 us
    all_to_all x1, waiting for transfers between devices, shards(): lax.all_to_all(feat_grad.reshape(seg_rows, 1, head_cols), 'head', split_a...  13.1 us
    all_to_all x1, waiting for transfers between devices, shards(): lax.all_to_all(outbound_write, 'head', split_axis=1, concat_axis=0, tiled...  12.4 us
    all_to_all x1, blocking collectives, shards(): lax.all_to_all(decay_send, 'head', split_axis=1, concat_axis=0, tiled=True)  11.9 us
    all_to_all x1, waiting for transfers between devices, shards(): lax.all_to_all(feat_send, 'head', split_axis=1, concat_axis=0, tiled=True)  10.5 us
  transfers between devices with their start and end apart: 14, of which 14 were waited for; matrix products, arithmetic and copies ran while one was open for 13% of the time, Pallas kernels for 0%

commit v1 on v0

v1 whole, which is shorter than its diff:
```python
import jax
import jax.numpy as jnp
from jax import lax
from jax.sharding import PartitionSpec as P

PRECISE = lax.Precision.HIGH


def dot(spec, a, b):
    return jnp.einsum(spec, a, b, precision=PRECISE)


def shards(grad_out, features, step_size, log_decay, write_proj, read_proj):
    owners = lax.axis_size("head")
    segs = lax.axis_size("seq")
    q, heads = step_size.shape
    p = grad_out.shape[1] // heads
    groups, n = write_proj.shape[1:]
    per = heads // groups
    mine = heads // owners
    here = lax.axis_index("head")
    seg = lax.axis_index("seq")

    cum = jnp.cumsum(log_decay, axis=0)
    end = cum[-1]
    ends = lax.all_gather(end, ("seq", "head"))
    dy = grad_out.reshape(q, groups, per, p)
    x = features.reshape(q, groups, per, p)
    cum_g = cum.reshape(q, groups, per)
    dt_g = step_size.reshape(q, groups, per)
    from_start = jnp.exp(cum_g)
    to_end = jnp.exp(cum_g[-1:] - cum_g)
    x_in = x * (dt_g * to_end)[..., None]
    dy_in = dy * from_start[..., None]
    fwd = dot("qgn,qghp->ghnp", write_proj, x_in)
    adj = dot("qgn,qghp->ghnp", read_proj, dy_in)
    both = jnp.stack([fwd, adj]).reshape(2, owners, mine, n, p)
    got = lax.all_to_all(both, "head", split_axis=1, concat_axis=1, tiled=True)

    t = jnp.arange(q)
    causal = t[:, None] >= t[None, :]
    ct = jnp.moveaxis(cum_g, 0, 2)
    mat = jnp.exp(jnp.where(causal, ct[..., :, None] - ct[..., None, :], -jnp.inf))
    weighted = (dot("tghp,sghp->ghts", dy, x) * mat * jnp.moveaxis(dt_g, 0, 2)[:, :, None, :]).sum(1)
    matches = dot("tgn,sgn->gts", read_proj, write_proj)[:, None] * mat
    read_grad = dot("gts,sgn->tgn", weighted, write_proj)
    write_grad = dot("gts,tgn->sgn", weighted, read_proj)
    feat_grad = dot("ghts,tghp->sghp", matches, dy)

    logs = lax.dynamic_slice_in_dim(ends, here * mine, mine, 1).reshape(segs, owners, mine)
    seg_log = logs.sum(1)
    dec = jnp.exp(lax.dynamic_index_in_dim(logs, seg, 0, False))[:, :, None, None]
    zero = jnp.zeros((mine, n, p), jnp.float32)
    tf, ta = zero, zero
    for i in range(owners):
        tf = dec[i] * tf + got[0, i]
        k = owners - 1 - i
        ta = dec[k] * ta + got[1, k]
    totals = lax.all_gather(jnp.stack([tf, ta]), "seq")
    sd = jnp.exp(seg_log)[:, :, None, None]
    inc, out = zero, zero
    for s in range(segs - 1):
        inc = jnp.where(s < seg, sd[s] * inc + totals[s, 0], inc)
        k = segs - 1 - s
        out = jnp.where(k > seg, sd[k] * out + totals[k, 1], out)
    enters, leaves = [], []
    for i in range(owners):
        enters.append(inc)
        inc = dec[i] * inc + got[0, i]
        k = owners - 1 - i
        leaves.append(out)
        out = dec[k] * out + got[1, k]
    back = jnp.stack([jnp.stack(enters), jnp.stack(leaves[::-1])])
    back = lax.all_to_all(back, "head", split_axis=1, concat_axis=1, tiled=True)
    back = back.reshape(2, groups, per, n, p)

    read_grad = read_grad + dot("tghp,ghnp->tgn", dy_in, back[0])
    write_grad = write_grad + dot("sghp,ghnp->sgn", x_in, back[1])
    feat_grad = feat_grad + to_end[..., None] * dot("sgn,ghnp->sghp", write_proj, back[1])
    feat_grad = feat_grad * dt_g[..., None]
    return feat_grad.reshape(q, heads * p), write_grad, read_grad


def solution(mesh):
    wide = P(("seq", "head"), None)
    deep = P(("seq", "head"), None, None)
    return jax.shard_map(
        shards,
        mesh=mesh,
        in_specs=(wide, wide, wide, wide, deep, deep),
        out_specs=(wide, deep, deep),
        check_vma=False,
    )
```

time: 199 us -> 120 us (0.60)
  waiting for transfers between devices: 102 us -> 23 us
  blocking collectives: 11.9 us -> 65.8 us
  starting transfers between devices: 43 us -> 9.87 us
  matrix products: 20.8 us -> 8.07 us
  local copies, waits for them, and re-layouts: 14.6 us -> 10.3 us
  other arithmetic: 4.14 us -> 1.75 us
    all_gather x0 -> x2, blocking collectives: none -> 65.8 us  [the longest x1 55.5 us: shards(): ends = lax.all_gather(end, ('seq', 'head'))]
    all_to_all x8 -> x2, waiting for transfers between devices: 85 us -> 23 us  [the longest x1 23 us: shards(): back = lax.all_to_all(back, 'head', split_axis=1, concat_axis=1, tiled=True)]
    all_to_all x8 -> x2, starting transfers between devices: 28.1 us -> 9.87 us  [the longest x1 6.32 us: shards(): got = lax.all_to_all(both, 'head', split_axis=1, concat_axis=1, tiled=True)]
    ppermute x6 -> x0, waiting for transfers between devices: 17.1 us -> none  [shifted(): return lax.ppermute(block, axis, route)]
    ppermute x6 -> x0, starting transfers between devices: 14.9 us -> none  [shifted(): return lax.ppermute(block, axis, route)]
    dot_general x10, matrix products: 20.8 us -> 8.07 us  [dot(): return jnp.einsum(spec, a, b, precision=PRECISE)]
    all_to_all x1 -> x0, blocking collectives: 11.9 us -> none  [shards(): lax.all_to_all(decay_send, 'head', split_axis=1, concat_axis=0, tiled=True)]
    reshape x6 -> x0, local copies, waits for them, and re-layouts: 2.98 us -> none  [the longest x2 2.45 us: shards(): feat_grad.reshape(seg_rows, 1, head_cols)]
  transfers between devices with their start and end apart: 14 -> 2, of which waited for: 14 -> 1; matrix products, arithmetic and copies ran while one was open for 13% -> 4% of each run, Pallas kernels for 0% -> 0%
where the time goes in v1:
time: 120 us
  blocking collectives  65.8 us (55%)
  waiting for transfers between devices  23 us (19%)
  local copies, waits for them, and re-layouts  10.3 us (9%)
  starting transfers between devices  9.87 us (8%)
  matrix products  8.07 us (7%)
  other arithmetic  1.75 us (1%)
    all_gather x1, blocking collectives, shards(): ends = lax.all_gather(end, ('seq', 'head'))  55.5 us
    all_to_all x1, waiting for transfers between devices, shards(): back = lax.all_to_all(back, 'head', split_axis=1, concat_axis=1, tiled=True)  23 us
    all_gather x1, blocking collectives, shards(): totals = lax.all_gather(jnp.stack([tf, ta]), 'seq')  10.3 us
    dot_general x10, matrix products, dot(): return jnp.einsum(spec, a, b, precision=PRECISE)  8.07 us
    unnamed x24, local copies, waits for them, and re-layouts  7.68 us
    all_to_all x1, starting transfers between devices, shards(): got = lax.all_to_all(both, 'head', split_axis=1, concat_axis=1, tiled=True)  6.32 us
    all_to_all x1, starting transfers between devices, shards(): back = lax.all_to_all(back, 'head', split_axis=1, concat_axis=1, tiled=True)  3.56 us
  transfers between devices with their start and end apart: 2, of which 1 were waited for; matrix products, arithmetic and copies ran while one was open for 4% of the time, Pallas kernels for 0%

profile of v1, /device:TPU:0, one launch (start us, length us, event | category | flops | bytes accessed | tf_op | source)
XLA Modules:
  0.0 119.8 jit_solution(9694501104899278258)
XLA Ops:
  0.6 0.9 copy.85
  1.8 1.3 %copy.89 = f32[128,1024]{0,1:T(8,128)S(1)} copy(f32[128,1024]{1,0:T(8,128)} %param.7) | data formatting | bytes 1048576 | tf_op args[1]
  3.4 0.5 copy-done.5
  4.0 0.5 convolution_bitcast_fusion.7
  4.4 0.6 copy-done.1
  5.0 0.5 convolution_bitcast_fusion.6
  5.6 1.1 copy.92
  6.7 6.3 %all-to-all-start = ((f32[2,8,2,128,64]{3,4,2,0,1:T(8,128)}), f32[2,8,2,128,64]{3,4,2,0,1:T(8,128)S(1)}, u32[]{:S(2)}, u32[]{:S(2)}) async-start(f32[2,8,2,128,64]{3,4,2,0,1:T(8,128)} %copy.92), calls=%async_computation | async-start | bytes 2097152 | tf_op jit(solution)/shard_map/all_to_all | solution.py:38
  13.0 55.5 %all-gather.1 = f32[32,1,16]{2,1,0:T(1,128)S(1)} all-gather(f32[1,1,16]{2,1,0:T(1,128)S(1)} %get-tuple-element.46), channel_id=1, replica_groups=mesh['seq'=4,'head'=8] {'seq','head'}, dimensions={0}, use_global_device_ids=true | all-gather | bytes 2112 | tf_op jit(solution)/shard_map/all_gather | solution.py:26
  69.5 10.3 %all-gather = f32[8,2,128,64]{2,3,1,0:T(8,128)S(1)} all-gather(f32[2,2,128,64]{2,3,1,0:T(8,128)S(1)} %pad_maximum_fusion.2), channel_id=2, replica_groups=mesh['seq'=4,'head'=8] {'seq'}, dimensions={0}, use_global_device_ids=true | all-gather | bytes 655360 | tf_op jit(solution)/shard_map/all_gather | solution.py:59
  80.8 1.1 copy.108
  81.9 3.6 %all-to-all-start.1 = ((f32[2,8,2,128,64]{3,4,2,0,1:T(8,128)}), f32[2,8,2,128,64]{3,4,2,0,1:T(8,128)S(1)}, u32[]{:S(2)}, u32[]{:S(2)}) async-start(f32[2,8,2,128,64]{3,4,2,0,1:T(8,128)} %copy.108), calls=%async_computation.1 | async-start | bytes 2097152 | tf_op jit(solution)/shard_map/all_to_all | solution.py:74
  85.5 2.0 %fusion.1 = f32[8,128,128]{2,1,0:T(8,128)} fusion(f32[128,8,2,64]{0,3,2,1:T(8,128)S(1)} %bitcast.281, f32[128,8,2,64]{0,3,2,1:T(8,128)S(1)} %bitcast.285, f32[8,2,128]{2,1,0:T(2,128)S(1)} %bitcast.299, f32[8,2,128]{2,1,0:T(2,128)S(1)} %bitcast.294, pred[128,128]{1,0:T(8,128)(4,1)S(1)} %iota_compare_fusion), kind=kOutput, calls=%fused_computation.2 | convolution fusion | flops 101842944 | bytes 1605632 | tf_op jit(solution)/shard_map/tghp,sghp->ghts/dot_general | solution.py:10
  87.5 1.5 %fusion.17 = f32[8,128,128]{2,1,0:T(8,128)} fusion(f32[128,8,128]{2,1,0:T(8,128)S(1)} %copy-done, f32[128,8,128]{2,1,0:T(8,128)S(1)} %copy-done.1), kind=kOutput, calls=%fused_computation.31 | convolution fusion | flops 100663296 | bytes 1572864 | tf_op jit(solution)/shard_map/tgn,sgn->gts/dot_general | solution.py:10
  89.0 23.0 %all-to-all-done.1 = f32[2,8,2,128,64]{3,4,2,0,1:T(8,128)S(1)} async-done(((f32[2,8,2,128,64]{3,4,2,0,1:T(8,128)}), f32[2,8,2,128,64]{3,4,2,0,1:T(8,128)S(1)}, u32[]{:S(2)}, u32[]{:S(2)}) %all-to-all-start.1) | async-done | bytes 1048608 | tf_op jit(solution)/shard_map/all_to_all | solution.py:74
  112.0 0.6 convolution_bitcast_fusion.3
  113.0 0.6 fusion.5
  113.6 1.1 copy.118
  114.7 0.6 convolution_bitcast_fusion.1
  115.3 0.5 fusion.4
  115.8 1.1 copy.119
  116.9 0.7 fusion.6
  117.9 0.8 fusion.3
  118.8 1.0 copy.117
  (46 shorter events, 3.4 us)
Async XLA Ops:
  0.6 3.3 %copy-start = (f32[128,8,128]{2,1,0:T(8,128)S(1)}, f32[128,8,128]{2,1,0:T(8,128)}, u32[]{:S(2)}) copy-start(f32[128,8,128]{2,1,0:T(8,128)} %param.10) | copy-start | bytes 1572868
  1.8 1.3 %copy-start.4 = (f32[128,1024]{1,0:T(8,128)S(1)}, f32[128,1024]{1,0:T(8,128)}, u32[]{:S(2)}) copy-start(f32[128,1024]{1,0:T(8,128)} %param.6) | copy-start | bytes 1572868
  3.2 0.7 copy-start.5
  4.0 1.0 copy-start.1
  6.7 62.6 %all-to-all-start = ((f32[2,8,2,128,64]{3,4,2,0,1:T(8,128)}), f32[2,8,2,128,64]{3,4,2,0,1:T(8,128)S(1)}, u32[]{:S(2)}, u32[]{:S(2)}) async-start(f32[2,8,2,128,64]{3,4,2,0,1:T(8,128)} %copy.92), calls=%async_computation | async-start | bytes 2097152 | tf_op jit(solution)/shard_map/all_to_all | solution.py:38
  81.9 30.1 %all-to-all-start.1 = ((f32[2,8,2,128,64]{3,4,2,0,1:T(8,128)}), f32[2,8,2,128,64]{3,4,2,0,1:T(8,128)S(1)}, u32[]{:S(2)}, u32[]{:S(2)}) async-start(f32[2,8,2,128,64]{3,4,2,0,1:T(8,128)} %copy.108), calls=%async_computation.1 | async-start | bytes 2097152 | tf_op jit(solution)/shard_map/all_to_all | solution.py:74
  112.0 1.0 copy-start.3
  116.9 1.0 copy-start.2

commit v2 on v1

v2 whole, which is shorter than its diff:
```python
import functools

import jax
import jax.numpy as jnp
from jax import lax
from jax.experimental import pallas as pl
from jax.experimental.pallas import tpu as pltpu
from jax.sharding import PartitionSpec as P

MESH = pl.DeviceIdType.MESH
CORES = 2
EXTRA = 8


def split(a):
    high = a.astype(jnp.bfloat16)
    return high, (a - high.astype(jnp.float32)).astype(jnp.bfloat16)


def dot3(a, b, left, right):
    dims = (((left,), (right,)), ((), ()))

    def one(u, v):
        return lax.dot_general(u, v, dims, preferred_element_type=jnp.float32)

    return one(a[0], b[0]) + (one(a[0], b[1]) + one(a[1], b[0]))


def kernel(
    segs, nz, dy_ref, x_ref, dt_ref, la_ref, b_ref, c_ref, feat_ref, write_ref, read_ref,
    send, keep, other, chip, got, total, peers, running, enter, back, back2, xin_ref, dyin_ref,
    ps, pr, zs, zr, ss, sr, bs, br, qs, qr,
):
    q, heads = dt_ref.shape
    groups, n = b_ref.shape[1:]
    per = heads // groups
    p = dy_ref.shape[1] // heads
    lanes = per * p
    gpo = groups // nz
    seg = lax.axis_index("seq")
    head = lax.axis_index("head")
    z, core = head // CORES, lax.rem(head, CORES)
    forward = core == 1
    partner = (seg, z * CORES + (1 - core))

    def along_z(k):
        return lax.rem(z + k + nz, nz)

    def along_seq(k):
        return lax.rem(seg + k + segs, segs)

    def at_z(other_z):
        return (seg, other_z * CORES + core)

    barrier = pltpu.get_barrier_semaphore()
    pl.semaphore_signal(barrier, inc=1, device_id=partner, device_id_type=MESH)
    for k in range(1, nz):
        pl.semaphore_signal(barrier, inc=1, device_id=at_z(along_z(k)), device_id_type=MESH)
    for k in range(1, segs):
        pl.semaphore_signal(barrier, inc=1, device_id=(along_seq(k), head), device_id_type=MESH)

    def copy(src, dst, s_sem, r_sem, device):
        return pltpu.make_async_remote_copy(
            src_ref=src, dst_ref=dst, send_sem=s_sem, recv_sem=r_sem,
            device_id=device, device_id_type=MESH,
        )

    rows = lax.broadcasted_iota(jnp.int32, (q, q), 0)
    cols = lax.broadcasted_iota(jnp.int32, (q, q), 1)
    causal = rows >= cols
    tri = causal.astype(jnp.float32)
    cum = jnp.dot(tri, la_ref[...], precision=lax.Precision.HIGHEST,
                  preferred_element_type=jnp.float32)
    dt = dt_ref[...]
    turned = jnp.concatenate(
        [cum, dt, jnp.zeros((q, q - 2 * heads), jnp.float32)], axis=1).T

    def spread(a, g):
        return jnp.concatenate(
            [jnp.broadcast_to(a[:, h:h + 1], (a.shape[0], p))
             for h in range(g * per, (g + 1) * per)], axis=1)

    def cut(g):
        return slice(g * lanes, (g + 1) * lanes)

    for g in range(groups):
        cum_l = spread(cum, g)
        end_l = cum_l[q - 1:q, :]
        x_in = x_ref[:, cut(g)] * (spread(dt, g) * jnp.exp(end_l - cum_l))
        dy_in = dy_ref[:, cut(g)] * jnp.exp(cum_l)
        xin_ref[:, cut(g)] = x_in
        dyin_ref[:, cut(g)] = dy_in
        fwd = dot3(split(b_ref[:, g, :]), split(x_in), 0, 0)
        adj = dot3(split(c_ref[:, g, :]), split(dy_in), 0, 0)
        log = jnp.broadcast_to(end_l, (EXTRA, lanes))
        send[g, :n, :] = jnp.where(forward, adj, fwd)
        send[g, n:, :] = log
        keep[g, :n, :] = jnp.where(forward, fwd, adj)
        keep[g, n:, :] = log
        if g == 0:
            pl.semaphore_wait(barrier, nz + segs - 1)
        copy(send.at[g], other.at[g], ps.at[g], pr.at[g], partner).start()

    def decayed(log, state, add):
        return jnp.exp(log[0:1, :]) * state + add

    for k in list(range(1, nz)) + [0]:
        owner = along_z(k)
        for j in range(gpo):
            g = owner * gpo + j
            copy(send.at[g], other.at[g], ps.at[g], pr.at[g], partner).wait_recv()
            state = decayed(keep[g, n:, :], other[g, :n, :], keep[g, :n, :])
            log = keep[g, n:, :] + other[g, n:, :]
            if k == 0:
                got[z, j, :n, :] = state
                got[z, j, n:, :] = log
            else:
                chip[g, :n, :] = state
                chip[g, n:, :] = log
                copy(chip.at[g], got.at[z, j], zs.at[k, j], zr.at[z, j], at_z(owner)).start()

    for g in range(groups):
        bs_g, cs_g = split(b_ref[:, g, :]), split(c_ref[:, g, :])
        pairs = dot3(cs_g, bs_g, 1, 1)
        weighted = jnp.zeros((q, q), jnp.float32)
        parts = []
        for h in range(g * per, (g + 1) * per):
            mat = jnp.exp(jnp.where(causal, cum[:, h:h + 1] - turned[h:h + 1, :], -jnp.inf))
            dy_h = split(dy_ref[:, h * p:(h + 1) * p])
            x_h = split(x_ref[:, h * p:(h + 1) * p])
            weighted += dot3(dy_h, x_h, 1, 1) * (mat * turned[heads + h:heads + h + 1, :])
            parts.append(dot3(split(pairs * mat), dy_h, 0, 0))
        w = split(weighted)
        read_ref[:, g, :] = dot3(w, bs_g, 1, 0)
        write_ref[:, g, :] = dot3(w, cs_g, 0, 0)
        feat_ref[:, cut(g)] = jnp.concatenate(parts, axis=1)

    for k in range(1, nz):
        src = along_z(-k)
        for j in range(gpo):
            copy(chip.at[j], got.at[src, j], zs.at[k, j], zr.at[src, j], at_z(src)).wait_recv()

    def place(i):
        return jnp.where(forward, i, nz - 1 - i)

    for j in range(gpo):
        state = got[place(0), j, :n, :]
        log = got[place(0), j, n:, :]
        for i in range(1, nz):
            state = decayed(got[place(i), j, n:, :], state, got[place(i), j, :n, :])
            log = log + got[place(i), j, n:, :]
        total[j, :n, :] = state
        total[j, n:, :] = log

    def feeds(src, dst):
        return jnp.where(forward, dst - src, src - dst) > 0

    for k in range(1, segs):
        dst = along_seq(k)

        @pl.when(feeds(seg, dst))
        def _(k=k, dst=dst):
            copy(total, peers.at[seg], ss.at[k], sr.at[seg], (dst, head)).start()

    running[...] = jnp.zeros_like(running)
    for i in range(segs - 1):
        src = jnp.where(forward, i, segs - 1 - i)

        @pl.when(feeds(src, seg))
        def _(src=src):
            copy(total, peers.at[src], ss.at[0], sr.at[src], (src, head)).wait_recv()
            for j in range(gpo):
                running[j] = decayed(peers[src, j, n:, :], running[j], peers[src, j, :n, :])

    for j in range(gpo):
        state = running[j]
        for i in range(nz):
            enter[place(i), j] = state
            if i < nz - 1:
                state = decayed(got[place(i), j, n:, :], state, got[place(i), j, :n, :])
    for k in range(1, nz):
        dst = along_z(k)
        for j in range(gpo):
            copy(enter.at[dst, j], back.at[z * gpo + j], bs.at[k, j], br.at[z, j],
                 at_z(dst)).start()
    for j in range(gpo):
        back[z * gpo + j] = enter[z, j]
    for k in range(nz):
        src = along_z(-k)
        for j in range(gpo):
            g = src * gpo + j
            if k > 0:
                copy(enter.at[src, j], back.at[g], bs.at[k, j], br.at[src, j],
                     at_z(src)).wait_recv()
            copy(back.at[g], back2.at[g], qs.at[g], qr.at[g], partner).start()

    for g in range(groups):
        copy(back.at[g], back2.at[g], qs.at[g], qr.at[g], partner).wait_recv()
        own = decayed(other[g, n:, :], back[g], other[g, :n, :])
        theirs = back2[g]
        enters = split(jnp.where(forward, own, theirs))
        leaves = split(jnp.where(forward, theirs, own))
        cum_l = spread(cum, g)
        to_end = jnp.exp(cum_l[q - 1:q, :] - cum_l)
        read_ref[:, g, :] += dot3(split(dyin_ref[:, cut(g)]), enters, 1, 1)
        write_ref[:, g, :] += dot3(split(xin_ref[:, cut(g)]), leaves, 1, 1)
        feat_ref[:, cut(g)] = spread(dt, g) * (
            feat_ref[:, cut(g)] + to_end * dot3(split(b_ref[:, g, :]), leaves, 1, 0))

    for g in range(groups):
        copy(send.at[g], other.at[g], ps.at[g], pr.at[g], partner).wait_send()
        copy(back.at[g], back2.at[g], qs.at[g], qr.at[g], partner).wait_send()
    for k in range(1, nz):
        dst = along_z(k)
        for j in range(gpo):
            copy(chip.at[dst * gpo + j], got.at[z, j], zs.at[k, j], zr.at[z, j],
                 at_z(dst)).wait_send()
            copy(enter.at[dst, j], back.at[z * gpo + j], bs.at[k, j], br.at[z, j],
                 at_z(dst)).wait_send()
    for k in range(1, segs):
        dst = along_seq(k)

        @pl.when(feeds(seg, dst))
        def _(k=k, dst=dst):
            copy(total, peers.at[seg], ss.at[k], sr.at[seg], (dst, head)).wait_send()


def shards(segs, owners, *args):
    grad_out, _, step_size, _, write_proj, _ = args
    q, heads = step_size.shape
    groups, n = write_proj.shape[1:]
    lanes = grad_out.shape[1] // groups
    nz = owners // CORES
    gpo = groups // nz
    f32 = jnp.float32
    tall = n + EXTRA
    dma = pltpu.SemaphoreType.DMA
    vmem = pl.BlockSpec(memory_space=pltpu.VMEM)
    return pl.pallas_call(
        functools.partial(kernel, segs, nz),
        out_shape=(
            jax.ShapeDtypeStruct(grad_out.shape, f32),
            jax.ShapeDtypeStruct(write_proj.shape, f32),
            jax.ShapeDtypeStruct(write_proj.shape, f32),
        ),
        in_specs=[vmem] * 6,
        out_specs=(vmem,) * 3,
        scratch_shapes=[
            pltpu.VMEM((groups, tall, lanes), f32),
            pltpu.VMEM((groups, tall, lanes), f32),
            pltpu.VMEM((groups, tall, lanes), f32),
            pltpu.VMEM((groups, tall, lanes), f32),
            pltpu.VMEM((nz, gpo, tall, lanes), f32),
            pltpu.VMEM((gpo, tall, lanes), f32),
            pltpu.VMEM((segs, gpo, tall, lanes), f32),
            pltpu.VMEM((gpo, n, lanes), f32),
            pltpu.VMEM((nz, gpo, n, lanes), f32),
            pltpu.VMEM((groups, n, lanes), f32),
            pltpu.VMEM((groups, n, lanes), f32),
            pltpu.VMEM(grad_out.shape, f32),
            pltpu.VMEM(grad_out.shape, f32),
            dma((groups,)), dma((groups,)),
            dma((nz, gpo)), dma((nz, gpo)),
            dma((segs,)), dma((segs,)),
            dma((nz, gpo)), dma((nz, gpo)),
            dma((groups,)), dma((groups,)),
        ],
        compiler_params=pltpu.CompilerParams(
            collective_id=0, has_side_effects=True, vmem_limit_bytes=48 * 1024 * 1024,
        ),
    )(*args)


def solution(mesh):
    wide = P(("seq", "head"), None)
    deep = P(("seq", "head"), None, None)
    return jax.shard_map(
        functools.partial(shards, mesh.shape["seq"], mesh.shape["head"]),
        mesh=mesh,
        in_specs=(wide, wide, wide, wide, deep, deep),
        out_specs=(wide, deep, deep),
        check_vma=False,
    )
```

time: 120 us -> 52.7 us (0.44)
  the two profiles are of different devices: /device:TPU:0 before, /device:TPU:29 now
where the time goes in v2:
time: 52.7 us; the launch traced here: 52.3 us
  Pallas kernels  44.2 us (84%)
  local copies, waits for them, and re-layouts  7.45 us (14%)
  between operations  0.66 us (1%)
    pallas_call x1, Pallas kernels, shards(): pl.pallas_call(functools.partial(kernel, segs, nz), out_shape=(jax.ShapeD...  44.2 us
    unnamed x15, local copies, waits for them, and re-layouts  7.45 us

profile of v2, /device:TPU:29, one launch (start us, length us, event | category | flops | bytes accessed | tf_op | source)
XLA Modules:
  0.0 52.3 jit_solution(11093775031004310144)
XLA Ops:
  0.6 0.0 copy-start.4
  0.6 0.8 %copy.9.dt_ref = f32[128,16]{1,0:T(8,128)S(1)} copy(f32[128,16]{0,1:T(8,128)} %param.8) | data formatting | bytes 16384 | tf_op args[2]
  1.4 0.0 copy-done.4
  1.4 0.1 copy.10.la_ref
  1.5 0.0 copy-start
  1.6 1.0 %copy-done = f32[128,1024]{1,0:T(8,128)S(1)} copy-done((f32[128,1024]{1,0:T(8,128)S(1)}, f32[128,1024]{1,0:T(8,128)}, u32[]{:S(2)}) %copy-start) | copy-done | bytes 524312
  2.6 0.0 copy-start.1
  2.6 1.0 %copy-done.1 = f32[128,1024]{1,0:T(8,128)S(1)} copy-done((f32[128,1024]{1,0:T(8,128)S(1)}, f32[128,1024]{1,0:T(8,128)}, u32[]{:S(2)}) %copy-start.1) | copy-done | bytes 524312
  3.6 0.0 copy-start.2
  3.6 1.0 %copy-done.2 = f32[128,8,128]{2,1,0:T(8,128)S(1)} copy-done((f32[128,8,128]{2,1,0:T(8,128)S(1)}, f32[128,8,128]{2,1,0:T(8,128)}, u32[]{:S(2)}) %copy-start.2) | copy-done | bytes 524312
  4.7 0.0 copy-start.3
  4.7 1.0 %copy-done.3 = f32[128,8,128]{2,1,0:T(8,128)S(1)} copy-done((f32[128,8,128]{2,1,0:T(8,128)S(1)}, f32[128,8,128]{2,1,0:T(8,128)}, u32[]{:S(2)}) %copy-start.3) | copy-done | bytes 524312
  5.7 44.2 %shard_map.85 = (f32[128,1024]{1,0:T(8,128)S(1)}, f32[128,8,128]{2,1,0:T(8,128)S(1)}, f32[128,8,128]{2,1,0:T(8,128)S(1)}) custom-call(f32[128,1024]{1,0:T(8,128)S(1)} %copy-done, f32[128,1024]{1,0:T(8,128)S(1)} %copy-done.1, f32[128,16]{1,0:T(8,128)S(1)} %copy.9.dt_ref, f32[128,16]{1,0:T(8,128)S(1)} %copy.10.la_ref, f32[128,8,128]{2,1,0:T(8,128)S(1)} %copy-done.2, ...), custom_call_target="tpu_custom_call" | custom-call | tf_op jit(solution)/shard_map/pallas_call | solution.py:239
  50.0 0.8 %copy.14 = f32[128,1024]{1,0:T(8,128)} copy(f32[128,1024]{1,0:T(8,128)S(1)} %get-tuple-element.6) | data formatting | bytes 1048576
  50.8 0.8 %copy.15 = f32[128,8,128]{2,1,0:T(8,128)} copy(f32[128,8,128]{2,1,0:T(8,128)S(1)} %get-tuple-element.7) | data formatting | bytes 1048576
  51.5 0.8 %copy.16 = f32[128,8,128]{2,1,0:T(8,128)} copy(f32[128,8,128]{2,1,0:T(8,128)S(1)} %get-tuple-element.8) | data formatting | bytes 1048576
Async XLA Ops:
  0.6 0.8 %copy-start.4 = (f32[128,16]{0,1:T(8,128)S(1)}, f32[128,16]{0,1:T(8,128)}, u32[]{:S(2)}) copy-start(f32[128,16]{0,1:T(8,128)} %param.9) | copy-start | bytes 24580
  1.5 1.0 %copy-start = (f32[128,1024]{1,0:T(8,128)S(1)}, f32[128,1024]{1,0:T(8,128)}, u32[]{:S(2)}) copy-start(f32[128,1024]{1,0:T(8,128)} %dy_ref.1) | copy-start | bytes 1572868
  2.6 1.0 %copy-start.1 = (f32[128,1024]{1,0:T(8,128)S(1)}, f32[128,1024]{1,0:T(8,128)}, u32[]{:S(2)}) copy-start(f32[128,1024]{1,0:T(8,128)} %x_ref.1) | copy-start | bytes 1572868
  3.6 1.0 %copy-start.2 = (f32[128,8,128]{2,1,0:T(8,128)S(1)}, f32[128,8,128]{2,1,0:T(8,128)}, u32[]{:S(2)}) copy-start(f32[128,8,128]{2,1,0:T(8,128)} %b_ref.1) | copy-start | bytes 1572868
  4.7 1.0 %copy-start.3 = (f32[128,8,128]{2,1,0:T(8,128)S(1)}, f32[128,8,128]{2,1,0:T(8,128)}, u32[]{:S(2)}) copy-start(f32[128,8,128]{2,1,0:T(8,128)} %c_ref.1) | copy-start | bytes 1572868

commit v3 on v2

--- a/solution.py
+++ b/solution.py
@@ -27,11 +27,19 @@
 
 
 def kernel(
-    segs, nz, dy_ref, x_ref, dt_ref, la_ref, b_ref, c_ref, feat_ref, write_ref, read_ref,
+    segs, nz, dy_hbm, x_hbm, dt_ref, la_ref, b_hbm, c_hbm, feat_ref, write_ref, read_ref,
+    dy_ref, x_ref, b_ref, c_ref, loads,
     send, keep, other, chip, got, total, peers, running, enter, back, back2, xin_ref, dyin_ref,
     ps, pr, zs, zr, ss, sr, bs, br, qs, qr,
 ):
-    q, heads = dt_ref.shape
+    fetches = [
+        pltpu.make_async_copy(src, dst, loads.at[i])
+        for i, (src, dst) in enumerate(
+            [(x_hbm, x_ref), (b_hbm, b_ref), (dy_hbm, dy_ref), (c_hbm, c_ref)])
+    ]
+    for fetch in fetches:
+        fetch.start()
+    heads, q = dt_ref.shape
     groups, n = b_ref.shape[1:]
     per = heads // groups
     p = dy_ref.shape[1] // heads
@@ -68,12 +76,13 @@
     rows = lax.broadcasted_iota(jnp.int32, (q, q), 0)
     cols = lax.broadcasted_iota(jnp.int32, (q, q), 1)
     causal = rows >= cols
-    tri = causal.astype(jnp.float32)
-    cum = jnp.dot(tri, la_ref[...], precision=lax.Precision.HIGHEST,
-                  preferred_element_type=jnp.float32)
-    dt = dt_ref[...]
+    upto = (rows <= cols).astype(jnp.float32)
+    cum_t = jnp.dot(la_ref[...], upto, precision=lax.Precision.HIGHEST,
+                    preferred_element_type=jnp.float32)
     turned = jnp.concatenate(
-        [cum, dt, jnp.zeros((q, q - 2 * heads), jnp.float32)], axis=1).T
+        [cum_t, dt_ref[...], jnp.zeros((q - 2 * heads, q), jnp.float32)], axis=0)
+    upright = turned.T
+    cum, dt = upright[:, :heads], upright[:, heads:2 * heads]
 
     def spread(a, g):
         return jnp.concatenate(
@@ -83,7 +92,10 @@
     def cut(g):
         return slice(g * lanes, (g + 1) * lanes)
 
-    for g in range(groups):
+    def decayed(log, state, add):
+        return jnp.exp(log[0:1, :]) * state + add
+
+    def chunk_states(g):
         cum_l = spread(cum, g)
         end_l = cum_l[q - 1:q, :]
         x_in = x_ref[:, cut(g)] * (spread(dt, g) * jnp.exp(end_l - cum_l))
@@ -97,29 +109,40 @@
         send[g, n:, :] = log
         keep[g, :n, :] = jnp.where(forward, fwd, adj)
         keep[g, n:, :] = log
-        if g == 0:
+
+    def chip_state(g):
+        owner, j = g // gpo, g % gpo
+        copy(send.at[g], other.at[g], ps.at[g], pr.at[g], partner).wait_recv()
+        state = decayed(keep[g, n:, :], other[g, :n, :], keep[g, :n, :])
+        log = keep[g, n:, :] + other[g, n:, :]
+
+        @pl.when(z == owner)
+        def _():
+            got[z, j, :n, :] = state
+            got[z, j, n:, :] = log
+
+        @pl.when(z != owner)
+        def _():
+            chip[g, :n, :] = state
+            chip[g, n:, :] = log
+            copy(chip.at[g], got.at[z, j], zs.at[g], zr.at[z, j], at_z(owner)).start()
+
+    mixed = [o for pair in zip(range(nz // 2), range(nz // 2, nz)) for o in pair]
+    order = [o * gpo + j for j in range(gpo) for o in mixed]
+    lag = 2
+    for fetch in fetches:
+        fetch.wait()
+    for i, g in enumerate(order):
+        chunk_states(g)
+        if i == 0:
             pl.semaphore_wait(barrier, nz + segs - 1)
         copy(send.at[g], other.at[g], ps.at[g], pr.at[g], partner).start()
-
-    def decayed(log, state, add):
-        return jnp.exp(log[0:1, :]) * state + add
-
-    for k in list(range(1, nz)) + [0]:
-        owner = along_z(k)
-        for j in range(gpo):
-            g = owner * gpo + j
-            copy(send.at[g], other.at[g], ps.at[g], pr.at[g], partner).wait_recv()
-            state = decayed(keep[g, n:, :], other[g, :n, :], keep[g, :n, :])
-            log = keep[g, n:, :] + other[g, n:, :]
-            if k == 0:
-                got[z, j, :n, :] = state
-                got[z, j, n:, :] = log
-            else:
-                chip[g, :n, :] = state
-                chip[g, n:, :] = log
-                copy(chip.at[g], got.at[z, j], zs.at[k, j], zr.at[z, j], at_z(owner)).start()
-
-    for g in range(groups):
+        if i >= lag:
+            chip_state(order[i - lag])
+    for g in order[len(order) - lag:]:
+        chip_state(g)
+
+    def within(g):
         bs_g, cs_g = split(b_ref[:, g, :]), split(c_ref[:, g, :])
         pairs = dot3(cs_g, bs_g, 1, 1)
         weighted = jnp.zeros((q, q), jnp.float32)
@@ -135,15 +158,20 @@
         write_ref[:, g, :] = dot3(w, cs_g, 0, 0)
         feat_ref[:, cut(g)] = jnp.concatenate(parts, axis=1)
 
-    for k in range(1, nz):
-        src = along_z(-k)
-        for j in range(gpo):
-            copy(chip.at[j], got.at[src, j], zs.at[k, j], zr.at[src, j], at_z(src)).wait_recv()
-
     def place(i):
         return jnp.where(forward, i, nz - 1 - i)
 
+    def feeds(src, dst):
+        return jnp.where(forward, dst - src, src - dst) > 0
+
+    half, most = groups // 2, groups * 3 // 4
+    for g in range(half):
+        within(g)
+
     for j in range(gpo):
+        for k in range(1, nz):
+            src = along_z(-k)
+            copy(chip.at[j], got.at[src, j], zs.at[j], zr.at[src, j], at_z(src)).wait_recv()
         state = got[place(0), j, :n, :]
         log = got[place(0), j, n:, :]
         for i in range(1, nz):
@@ -151,50 +179,54 @@
             log = log + got[place(i), j, n:, :]
         total[j, :n, :] = state
         total[j, n:, :] = log
-
-    def feeds(src, dst):
-        return jnp.where(forward, dst - src, src - dst) > 0
-
-    for k in range(1, segs):
-        dst = along_seq(k)
-
-        @pl.when(feeds(seg, dst))
-        def _(k=k, dst=dst):
-            copy(total, peers.at[seg], ss.at[k], sr.at[seg], (dst, head)).start()
+        for k in range(1, segs):
+            dst = along_seq(k)
+
+            @pl.when(feeds(seg, dst))
+            def _(k=k, dst=dst, j=j):
+                copy(total.at[j], peers.at[seg, j], ss.at[k, j], sr.at[seg, j],
+                     (dst, head)).start()
+
+    for g in range(half, most):
+        within(g)
 
     running[...] = jnp.zeros_like(running)
-    for i in range(segs - 1):
-        src = jnp.where(forward, i, segs - 1 - i)
-
-        @pl.when(feeds(src, seg))
-        def _(src=src):
-            copy(total, peers.at[src], ss.at[0], sr.at[src], (src, head)).wait_recv()
-            for j in range(gpo):
+    for j in range(gpo):
+        for i in range(segs - 1):
+            src = jnp.where(forward, i, segs - 1 - i)
+
+            @pl.when(feeds(src, seg))
+            def _(src=src, j=j):
+                copy(total.at[j], peers.at[src, j], ss.at[0, j], sr.at[src, j],
+                     (src, head)).wait_recv()
                 running[j] = decayed(peers[src, j, n:, :], running[j], peers[src, j, :n, :])
 
-    for j in range(gpo):
         state = running[j]
         for i in range(nz):
             enter[place(i), j] = state
             if i < nz - 1:
                 state = decayed(got[place(i), j, n:, :], state, got[place(i), j, :n, :])
-    for k in range(1, nz):
-        dst = along_z(k)
-        for j in range(gpo):
+        for k in range(1, nz):
+            dst = along_z(k)
             copy(enter.at[dst, j], back.at[z * gpo + j], bs.at[k, j], br.at[z, j],
                  at_z(dst)).start()
-    for j in range(gpo):
-        back[z * gpo + j] = enter[z, j]
-    for k in range(nz):
-        src = along_z(-k)
-        for j in range(gpo):
-            g = src * gpo + j
-            if k > 0:
-                copy(enter.at[src, j], back.at[g], bs.at[k, j], br.at[src, j],
-                     at_z(src)).wait_recv()
+        mine = z * gpo + j
+        back[mine] = enter[z, j]
+        copy(back.at[mine], back2.at[mine], qs.at[mine], qr.at[mine], partner).start()
+
+    for g in range(most, groups):
+        within(g)
+
+    def hand_on(g):
+        owner, j = g // gpo, g % gpo
+
+        @pl.when(z != owner)
+        def _():
+            copy(enter.at[owner, j], back.at[g], bs.at[1, j], br.at[owner, j],
+                 at_z(owner)).wait_recv()
             copy(back.at[g], back2.at[g], qs.at[g], qr.at[g], partner).start()
 
-    for g in range(groups):
+    def finish(g):
         copy(back.at[g], back2.at[g], qs.at[g], qr.at[g], partner).wait_recv()
         own = decayed(other[g, n:, :], back[g], other[g, :n, :])
         theirs = back2[g]
@@ -207,27 +239,38 @@
         feat_ref[:, cut(g)] = spread(dt, g) * (
             feat_ref[:, cut(g)] + to_end * dot3(split(b_ref[:, g, :]), leaves, 1, 0))
 
+    for i, g in enumerate(order):
+        hand_on(g)
+        if i >= lag:
+            finish(order[i - lag])
+    for g in order[len(order) - lag:]:
+        finish(g)
+
     for g in range(groups):
         copy(send.at[g], other.at[g], ps.at[g], pr.at[g], partner).wait_send()
         copy(back.at[g], back2.at[g], qs.at[g], qr.at[g], partner).wait_send()
-    for k in range(1, nz):
-        dst = along_z(k)
-        for j in range(gpo):
-            copy(chip.at[dst * gpo + j], got.at[z, j], zs.at[k, j], zr.at[z, j],
-                 at_z(dst)).wait_send()
+        owner, j = g // gpo, g % gpo
+
+        @pl.when(z != owner)
+        def _(g=g, owner=owner, j=j):
+            copy(chip.at[g], got.at[z, j], zs.at[g], zr.at[z, j], at_z(owner)).wait_send()
+
+    for j in range(gpo):
+        for k in range(1, nz):
+            dst = along_z(k)
             copy(enter.at[dst, j], back.at[z * gpo + j], bs.at[k, j], br.at[z, j],
                  at_z(dst)).wait_send()
-    for k in range(1, segs):
-        dst = along_seq(k)
-
-        @pl.when(feeds(seg, dst))
-        def _(k=k, dst=dst):
-            copy(total, peers.at[seg], ss.at[k], sr.at[seg], (dst, head)).wait_send()
+        for k in range(1, segs):
+            dst = along_seq(k)
+
+            @pl.when(feeds(seg, dst))
+            def _(k=k, dst=dst, j=j):
+                copy(total.at[j], peers.at[seg, j], ss.at[k, j], sr.at[seg, j],
+                     (dst, head)).wait_send()
 
 
 def shards(segs, owners, *args):
-    grad_out, _, step_size, _, write_proj, _ = args
-    q, heads = step_size.shape
+    grad_out, features, step_size, log_decay, write_proj, read_proj = args
     groups, n = write_proj.shape[1:]
     lanes = grad_out.shape[1] // groups
     nz = owners // CORES
@@ -236,6 +279,7 @@
     tall = n + EXTRA
     dma = pltpu.SemaphoreType.DMA
     vmem = pl.BlockSpec(memory_space=pltpu.VMEM)
+    whole = pl.BlockSpec(memory_space=pl.ANY)
     return pl.pallas_call(
         functools.partial(kernel, segs, nz),
         out_shape=(
@@ -243,9 +287,14 @@
             jax.ShapeDtypeStruct(write_proj.shape, f32),
             jax.ShapeDtypeStruct(write_proj.shape, f32),
         ),
-        in_specs=[vmem] * 6,
+        in_specs=[whole, whole, vmem, vmem, whole, whole],
         out_specs=(vmem,) * 3,
         scratch_shapes=[
+            pltpu.VMEM(grad_out.shape, f32),
+            pltpu.VMEM(grad_out.shape, f32),
+            pltpu.VMEM(write_proj.shape, f32),
+            pltpu.VMEM(write_proj.shape, f32),
+            dma((4,)),
             pltpu.VMEM((groups, tall, lanes), f32),
             pltpu.VMEM((groups, tall, lanes), f32),
             pltpu.VMEM((groups, tall, lanes), f32),
@@ -260,15 +309,15 @@
             pltpu.VMEM(grad_out.shape, f32),
             pltpu.VMEM(grad_out.shape, f32),
             dma((groups,)), dma((groups,)),
-            dma((nz, gpo)), dma((nz, gpo)),
-            dma((segs,)), dma((segs,)),
+            dma((groups,)), dma((nz, gpo)),
+            dma((segs, gpo)), dma((segs, gpo)),
             dma((nz, gpo)), dma((nz, gpo)),
             dma((groups,)), dma((groups,)),
         ],
         compiler_params=pltpu.CompilerParams(
-            collective_id=0, has_side_effects=True, vmem_limit_bytes=48 * 1024 * 1024,
+            collective_id=0, has_side_effects=True, vmem_limit_bytes=56 * 1024 * 1024,
         ),
-    )(*args)
+    )(grad_out, features, step_size.T, log_decay.T, write_proj, read_proj)
 
 
 def solution(mesh):

time: 52.7 us -> 40.9 us (0.78)
  the two profiles are of different devices: /device:TPU:29 before, /device:TPU:0 now
where the time goes in v3:
time: 40.9 us; the launch traced here: 40.4 us
  Pallas kernels  35.8 us (88%)
  local copies, waits for them, and re-layouts  3.97 us (10%)
  between operations  0.65 us (2%)
    pallas_call x1, Pallas kernels, shards(): pl.pallas_call(functools.partial(kernel, segs, nz), out_shape=(jax.ShapeD...  35.8 us
    unnamed x7, local copies, waits for them, and re-layouts  3.97 us

profile of v3, /device:TPU:0, one launch (start us, length us, event | category | flops | bytes accessed | tf_op | source)
XLA Modules:
  0.0 40.4 jit_solution(14010358787925191893)
XLA Ops:
  0.6 35.8 %shard_map.85 = (f32[128,1024]{1,0:T(8,128)}, f32[128,8,128]{2,1,0:T(8,128)}, f32[128,8,128]{2,1,0:T(8,128)}) custom-call(f32[128,1024]{1,0:T(8,128)} %dy_hbm.1, f32[128,1024]{1,0:T(8,128)} %x_hbm.1, f32[16,128]{1,0:T(8,128)} %bitcast.2, f32[16,128]{1,0:T(8,128)} %bitcast.3, f32[128,8,128]{2,1,0:T(8,128)} %b_hbm.1, f32[128,8,128]{2,1,0:T(8,128)} %c_hbm.1), custom_call_target="tpu_custom_call" | custom-call | tf_op jit(solution)/shard_map/pallas_call | solution.py:283
  36.5 0.0 copy-start.1
  36.5 1.9 %copy.12 = f32[128,1024]{1,0:T(8,128)} copy(f32[128,1024]{1,0:T(8,128)} %get-tuple-element.6) | data formatting | bytes 1048576
  38.4 0.0 copy-done.1
  38.4 0.0 copy-start
  38.4 0.8 %copy.13 = f32[128,8,128]{2,1,0:T(8,128)} copy(f32[128,8,128]{2,1,0:T(8,128)S(1)} %copy-done.1) | data formatting | bytes 1048576
  39.2 0.4 %copy-done = f32[128,8,128]{2,1,0:T(8,128)S(1)} copy-done((f32[128,8,128]{2,1,0:T(8,128)S(1)}, f32[128,8,128]{2,1,0:T(8,128)}, u32[]{:S(2)}) %copy-start) | copy-done | bytes 524312
  39.6 0.8 %copy.14 = f32[128,8,128]{2,1,0:T(8,128)} copy(f32[128,8,128]{2,1,0:T(8,128)S(1)} %copy-done) | data formatting | bytes 1048576
Async XLA Ops:
  36.5 2.0 %copy-start.1 = (f32[128,8,128]{2,1,0:T(8,128)S(1)}, f32[128,8,128]{2,1,0:T(8,128)}, u32[]{:S(2)}) copy-start(f32[128,8,128]{2,1,0:T(8,128)} %get-tuple-element.7) | copy-start | bytes 1572868
  38.4 1.2 %copy-start = (f32[128,8,128]{2,1,0:T(8,128)S(1)}, f32[128,8,128]{2,1,0:T(8,128)}, u32[]{:S(2)}) copy-start(f32[128,8,128]{2,1,0:T(8,128)} %get-tuple-element.8) | copy-start | bytes 1572868

commit v4 on v3

--- a/solution.py
+++ b/solution.py
@@ -269,6 +269,12 @@
                      (dst, head)).wait_send()
 
 
+def deliver(a_in, b_in, c_in, a_out, b_out, c_out):
+    a_out[...] = a_in[...]
+    b_out[...] = b_in[...]
+    c_out[...] = c_in[...]
+
+
 def shards(segs, owners, *args):
     grad_out, features, step_size, log_decay, write_proj, read_proj = args
     groups, n = write_proj.shape[1:]
@@ -280,7 +286,7 @@
     dma = pltpu.SemaphoreType.DMA
     vmem = pl.BlockSpec(memory_space=pltpu.VMEM)
     whole = pl.BlockSpec(memory_space=pl.ANY)
-    return pl.pallas_call(
+    grads = pl.pallas_call(
         functools.partial(kernel, segs, nz),
         out_shape=(
             jax.ShapeDtypeStruct(grad_out.shape, f32),
@@ -318,6 +324,19 @@
             collective_id=0, has_side_effects=True, vmem_limit_bytes=56 * 1024 * 1024,
         ),
     )(grad_out, features, step_size.T, log_decay.T, write_proj, read_proj)
+    steps = 2
+    blocks = [
+        pl.BlockSpec((g.shape[0] // steps,) + g.shape[1:], lambda i, r=g.ndim: (i,) + (0,) * (r - 1))
+        for g in grads
+    ]
+    return pl.pallas_call(
+        deliver,
+        grid=(steps,),
+        out_shape=tuple(jax.ShapeDtypeStruct(g.shape, f32) for g in grads),
+        in_specs=blocks,
+        out_specs=tuple(blocks),
+        compiler_params=pltpu.CompilerParams(vmem_limit_bytes=56 * 1024 * 1024),
+    )(*grads)
 
 
 def solution(mesh):

time: 40.9 us -> 39.3 us (0.961)
  local copies, waits for them, and re-layouts: 3.97 us -> 0 us
  Pallas kernels: 35.8 us -> 38.1 us
    unnamed x7 -> x0, local copies, waits for them, and re-layouts: 3.97 us -> none
    pallas_call x0 -> x1, Pallas kernels: none -> 2.31 us  [shards(): pl.pallas_call(deliver, grid=(steps,), out_shape=tuple((jax.ShapeDtypeStr...]
where the time goes in v4:
time: 39.3 us; the launch traced here: 38.8 us
  Pallas kernels  38.1 us (97%)
  between operations  0.64 us (2%)
    pallas_call x1, Pallas kernels, shards(): pl.pallas_call(functools.partial(kernel, segs, nz), out_shape=(jax.ShapeD...  35.8 us
    pallas_call x1, Pallas kernels, shards(): pl.pallas_call(deliver, grid=(steps,), out_shape=tuple((jax.ShapeDtypeStr...  2.31 us

profile of v4, /device:TPU:0, one launch (start us, length us, event | category | flops | bytes accessed | tf_op | source)
XLA Modules:
  0.0 38.8 jit_solution(17721760307550276444)
XLA Ops:
  0.6 35.8 %shard_map.85 = (f32[128,1024]{1,0:T(8,128)}, f32[128,8,128]{2,1,0:T(8,128)}, f32[128,8,128]{2,1,0:T(8,128)}) custom-call(f32[128,1024]{1,0:T(8,128)} %dy_hbm.1, f32[128,1024]{1,0:T(8,128)} %x_hbm.1, f32[16,128]{1,0:T(8,128)} %bitcast.2, f32[16,128]{1,0:T(8,128)} %bitcast.3, f32[128,8,128]{2,1,0:T(8,128)} %b_hbm.1, f32[128,8,128]{2,1,0:T(8,128)} %c_hbm.1), custom_call_target="tpu_custom_call" | custom-call | tf_op jit(solution)/shard_map/pallas_call | solution.py:289
  36.4 2.3 %shard_map.86 = (f32[128,1024]{1,0:T(8,128)}, f32[128,8,128]{2,1,0:T(8,128)}, f32[128,8,128]{2,1,0:T(8,128)}) custom-call(f32[128,1024]{1,0:T(8,128)} %get-tuple-element.6.a_in, f32[128,8,128]{2,1,0:T(8,128)} %get-tuple-element.7.b_in, f32[128,8,128]{2,1,0:T(8,128)} %get-tuple-element.8.c_in), custom_call_target="tpu_custom_call" | custom-call | tf_op jit(solution)/shard_map/pallas_call | solution.py:332
